TPU v7x, 512 devices: a whole 4x4x16 slice. The times are simulated.
512 devices in a mesh: seq: 32 (over x, z_lo), expert: 8 (over z_hi, y), mp: 2 (over core).
Axes of the slice: x: 4, y: 4, z: 16 (z_hi: 2, z_lo: 8; z = z_hi * 8 + z_lo), core: 2. Of those that a mesh axis runs over, the one named last changes fastest.
Arguments:
- queries: bfloat16 [8, 32, 128, 4096], P('expert', 'seq', None, 'mp'), may hold values from -6 to 6
- out_grad: bfloat16 [8, 32, 128, 4096], P('expert', 'seq', None, 'mp'), may hold values from -6 to 6
- prompt_kv: bfloat16 [8, 1024, 2, 256], P('expert', 'seq', None, 'mp'), may hold values from -6 to 6
- resp_kv: bfloat16 [8, 32, 128, 2, 256], P('expert', 'seq', None, None, 'mp'), may hold values from -6 to 6
- lengths: int32 [8, 32], P('expert', 'seq'), may hold values from 1 to 128, 3072 in all within a row
- grads: bfloat16 [8, 32, 128, 2048], P('expert', 'seq'), may hold values from -6 to 6
- routes: int32 [8, 32, 128, 8], P('expert', 'seq'), may hold values from 0 to 127, all different within a row; in each aligned block of 128 rows (0 to 127, 128 to 255, ..., all dimensions but the last counted through in order) at most 16 rows name the same one
- gates: float32 [8, 32, 128, 8], P('expert', 'seq'), may hold values from 0.1 to 1
- down_weight: bfloat16 [8, 1536, 2048], P('expert', 'mp'), may hold values from -0.125 to 0.125
Outputs:
- prompt_dkv: float32 [8, 1024, 2, 256], P('expert', 'seq', None, 'mp')
- resp_dkv: float32 [8, 32, 128, 2, 256], P('expert', 'seq', None, None, 'mp')
- expert_grad: bfloat16 [32, 8, 8, 16, 1536], P('seq', None, 'expert', None, 'mp')
Inputs may be any that keep to these rules, and one draw needn't show every extreme that they name: `routes`: the 8 experts of a token differ; among the rows of one device no expert is named by more than 16 rows.
All inputs are finite; a program needn't handle non-finite values. No bound on the sum of `lengths` on one device may be relied on, other than what follows from the above.
Results may differ from a plain program's by a relative error of at most 0.0049.
Values may be sent and summed in bfloat16 or wider, within the bound.
A program may use at most 64 MiB of HBM per device.

v0:
```python
import jax
import jax.numpy as jnp
from jax import lax
from jax.sharding import PartitionSpec as P

HD = 128


def local(queries, out_grad, prompt_kv, resp_kv, lengths, grads, routes, gates, down_weight):
    query_rows = queries[0, 0]
    row_count = query_rows.shape[0]
    kv_heads = resp_kv.shape[-1] // HD
    q_heads = query_rows.shape[-1] // HD
    group_size = q_heads // kv_heads
    score_scale = HD ** (-0.5)
    query_heads = query_rows.reshape(row_count, kv_heads, group_size, HD)
    gathered = lax.all_gather(prompt_kv, "seq", axis=1, tiled=True)
    prompt_len = gathered.shape[1]
    key_rows = jnp.concatenate([gathered[0, :, 0], resp_kv[0, 0, :, 0]], 0).reshape(
        -1, kv_heads, HD
    )
    value_rows = jnp.concatenate([gathered[0, :, 1], resp_kv[0, 0, :, 1]], 0).reshape(
        -1, kv_heads, HD
    )
    key_total = key_rows.shape[0]
    length = lengths[0, 0]
    position = jnp.arange(row_count)
    allowed = jnp.concatenate(
        [jnp.ones((row_count, prompt_len), jnp.bool_), position[None, :] <= position[:, None]], 1
    )
    scores = (
        jnp.einsum("icgd,jcd->cgij", query_heads, key_rows, preferred_element_type=jnp.float32)
        * score_scale
    )
    scores = jnp.where(allowed, scores, -jnp.inf)
    numerators = jnp.exp(scores - jnp.max(scores, -1, keepdims=True))
    attention = numerators / jnp.sum(numerators, -1, keepdims=True)
    attention_low = attention.astype(jnp.bfloat16)
    grad_out = out_grad[0, 0]
    grad_rows = jnp.where((position < length)[:, None], grad_out, jnp.zeros_like(grad_out))
    grad_heads = grad_rows.reshape(row_count, kv_heads, group_size, HD)
    grad_probs = jnp.einsum(
        "icgd,jcd->cgij", grad_heads, value_rows, preferred_element_type=jnp.float32
    )
    row_delta = jnp.sum(attention * grad_probs, -1, keepdims=True)
    grad_low = (attention * (grad_probs - row_delta) * score_scale).astype(jnp.bfloat16)
    grad_keys = jnp.einsum(
        "cgij,icgd->jcd", grad_low, query_heads, preferred_element_type=jnp.float32
    )
    grad_values = jnp.einsum(
        "cgij,icgd->jcd", attention_low, grad_heads, preferred_element_type=jnp.float32
    )
    every_term = jnp.stack(
        [
            grad_keys.reshape(key_total, kv_heads * HD),
            grad_values.reshape(key_total, kv_heads * HD),
        ],
        1,
    )
    prompt_part = lax.psum_scatter(every_term[:prompt_len], "seq", scatter_dimension=0, tiled=True)
    own_part = every_term[prompt_len:]
    token_rows = grads[0, 0]
    route_ids = routes[0, 0]
    gate_rows = gates[0, 0]
    local_experts = down_weight.shape[0]
    expert_devices = lax.axis_size("expert")
    capacity = row_count // 8
    expert_ids = jnp.arange(local_experts * expert_devices)
    matches = route_ids[:, :, None] == expert_ids[None, None, :]
    named_rows = jnp.any(matches, 1)
    valid_rows = (position < length).astype(jnp.float32)
    route_weight = (
        jnp.sum(jnp.where(matches, gate_rows[:, :, None], jnp.zeros_like(gate_rows[:, :, None])), 1)
        * valid_rows[:, None]
    )
    slot_index = jnp.cumsum(named_rows.astype(jnp.int32), 0) - 1
    selection = named_rows[:, :, None] & (
        slot_index[:, :, None] == jnp.arange(capacity)[None, None, :]
    )
    picked = jnp.einsum(
        "ixc,id->xcd",
        selection.astype(jnp.bfloat16),
        token_rows,
        preferred_element_type=jnp.float32,
    )
    slot_gate = jnp.einsum(
        "ixc,ix->xc", selection.astype(jnp.float32), route_weight, precision=lax.Precision.HIGHEST
    )
    outgoing = (
        (picked * slot_gate[:, :, None])
        .astype(jnp.bfloat16)
        .reshape(expert_devices, local_experts, capacity, token_rows.shape[1])
    )
    expert_grad = jnp.einsum(
        "sxcd,xfd->sxcf",
        lax.all_to_all(outgoing, "expert", split_axis=0, concat_axis=0, tiled=True),
        down_weight,
        preferred_element_type=jnp.float32,
    ).astype(jnp.bfloat16)
    return (prompt_part[None], own_part[None, None], expert_grad[None])


def solution(mesh):
    placed = (
        P("expert", "seq", None, "mp"),
        P("expert", "seq", None, "mp"),
        P("expert", "seq", None, "mp"),
        P("expert", "seq", None, None, "mp"),
        P("expert", "seq"),
        P("expert", "seq", None, None),
        P("expert", "seq", None, None),
        P("expert", "seq", None, None),
        P("expert", "mp", None),
    )
    return jax.shard_map(
        local,
        mesh=mesh,
        in_specs=placed,
        out_specs=(
            P("expert", "seq", None, "mp"),
            P("expert", "seq", None, None, "mp"),
            P("seq", None, "expert", None, "mp"),
        ),
        check_vma=False,
    )
```

profile of v0, /device:TPU:16, one launch (start us, length us, event | category | flops | bytes accessed | tf_op | source)
XLA Modules:
  0.0 430.9 jit_solution(1173876097495905706)
XLA Ops:
  7.2 0.0 copy-start
  8.0 0.5 iota_compare_fusion.3
  8.5 0.7 fusion.49
  9.2 0.1 copy.54
  9.3 0.2 reduce_window_sum.11
  9.5 0.7 select_reduce_fusion
  10.3 0.2 fusion.44
  10.5 2.1 fusion.21
  12.6 18.1 %all-to-all-start = ((bf16[8,1,16,2048]{3,2,1,0:T(8,128)(2,1)}), bf16[8,1,16,2048]{3,2,1,0:T(8,128)(2,1)}, u32[]{:S(2)}, u32[]{:S(2)}) async-start(bf16[8,1,16,2048]{3,2,1,0:T(8,128)(2,1)} %fusion.21), calls=%async_computation.1 | async-start | bytes 1048576 | tf_op jit(solution)/shard_map/all_to_all | solution.py:96
  30.6 0.0 reduce-scatter.2.cloned.1.call-start
  30.7 1.0 fusion.59
  31.7 0.7 copy.45
  32.4 134.5 %all_gather.3 = bf16[1,1024,2,128]{3,1,2,0:T(8,128)(2,1)S(1)} all-gather(bf16[1,32,2,128]{3,1,2,0:T(8,128)(2,1)S(1)} %copy.45), channel_id=1, replica_groups=mesh['seq'=32,'expert'=8,'mp'=2] {'seq'}, dimensions={1}, use_global_device_ids=true | all-gather | bytes 540672 | tf_op jit(solution)/shard_map/all_gather | solution.py:17
  166.9 0.7 slice_bitcast_fusion.1
  167.7 1.9 copy.68
  169.6 2.0 copy.64
  171.6 1.1 select_bitcast_fusion
  172.8 0.1 copy.69
  173.0 0.0 copy-start.4
  173.0 0.0 copy-start.6
  173.0 2.5 fusion.60
  175.5 1.2 fusion.5
  176.8 0.0 copy-done.4
  176.8 0.0 copy-done.6
  176.8 0.0 copy-start.5
  176.8 1.6 fusion.17
  178.4 0.0 copy-start.2
  178.4 0.0 copy-done.5
  178.4 0.0 copy-start.1
  178.4 2.2 fusion
  180.7 0.0 copy-done.1
  180.7 2.7 fusion.14
  183.3 0.0 copy-done.2
  183.4 0.0 copy-start.3
  183.4 0.8 copy-done.3
  184.2 1.1 fusion.28
  185.2 0.0 reduce-scatter.2.cloned.1.call-update
  185.3 0.9 fusion.42
  186.2 0.8 copy.58
  186.9 0.0 all-to-all-done
  186.9 0.0 copy-done
  186.9 2.9 fusion.25
  189.8 232.8 %reduce-scatter.2.cloned.1.call-done = f32[32,2,128]{2,0,1:T(8,128)} async-done(((f32[1024,2,128]{2,0,1:T(8,128)}), f32[32,2,128]{2,0,1:T(8,128)}) %reduce-scatter.2.cloned.1.call-update) | async-done | bytes 32784 | tf_op jit(solution)/shard_map/reduce_scatter | solution.py:60
  422.6 1.4 copy.57
  (7 shorter events, 0.1 us)
Async XLA Ops:
  7.2 179.8 %copy-start = (bf16[1,768,2048]{2,1,0:T(8,128)(2,1)S(1)}, bf16[1,768,2048]{2,1,0:T(8,128)(2,1)}, u32[]{:S(2)}) copy-start(bf16[1,768,2048]{2,1,0:T(8,128)(2,1)} %param.17) | copy-start | bytes 9437188
  12.6 174.3 %all-to-all-start = ((bf16[8,1,16,2048]{3,2,1,0:T(8,128)(2,1)}), bf16[8,1,16,2048]{3,2,1,0:T(8,128)(2,1)}, u32[]{:S(2)}, u32[]{:S(2)}) async-start(bf16[8,1,16,2048]{3,2,1,0:T(8,128)(2,1)} %fusion.21), calls=%async_computation.1 | async-start | bytes 1048576 | tf_op jit(solution)/shard_map/all_to_all | solution.py:96
  30.6 392.0 %reduce-scatter.2.cloned.1.call-start = ((), (), s32[]{:S(2)}) async-start(), calls=%async_computation.2 | async-start | bytes 1081344 | tf_op jit(solution)/shard_map/reduce_scatter | solution.py:60
  173.0 3.8 copy-start.4
  173.0 3.8 copy-start.6
  176.8 1.6 copy-start.5
  178.4 4.9 %copy-start.2 = (f32[1152,1,128]{2,0,1:T(8,128)}, f32[1152,1,128]{2,0,1:T(8,128)S(1)}, u32[]{:S(2)}) copy-start(f32[1152,1,128]{2,0,1:T(8,128)S(1)} %fusion.17) | copy-start | bytes 1769476
  178.4 2.3 copy-start.1
  183.4 0.8 copy-start.3
Sparse Core Ops, SparseCore 0:
  185.4 237.1 reduce-scatter.1
where the time goes:
time: 432 us; the launch traced here: 431 us
  waiting for transfers between devices  233 us (54%)
  blocking collectives  134 us (31%)
  starting transfers between devices  18.1 us (4%)
  between operations  15 us (3%)
  matrix products  14.2 us (3%)
  local copies, waits for them, and re-layouts  9.8 us (2%)
  other arithmetic  6.48 us (2%)
    reduce_scatter x1, waiting for transfers between devices, local(): lax.psum_scatter(every_term[:prompt_len], 'seq', scatter_dimension=0, til...  233 us
    all_gather x1, blocking collectives, local(): gathered = lax.all_gather(prompt_kv, 'seq', axis=1, tiled=True)  134 us
    all_to_all x1, starting transfers between devices, local(): lax.all_to_all(outgoing, 'expert', split_axis=0, concat_axis=0, tiled=True)  18.1 us
  transfers between devices with their start and end apart: 2, of which 1 were waited for; matrix products, arithmetic and copies ran while one was open for 5% of the time, Pallas kernels for 0%

commit v1 on v0

v1 whole, which is shorter than its diff:
```python
import functools
import math

import jax
import jax.numpy as jnp
from jax import lax
from jax.experimental import pallas as pl
from jax.experimental.pallas import tpu as pltpu
from jax.sharding import PartitionSpec as P

HD = 128
SCALE = HD**-0.5
SCALE2 = SCALE * math.log2(math.e)
MESH = pl.DeviceIdType.MESH
F32 = jnp.float32
BF16 = jnp.bfloat16
NT = (((1,), (1,)), ((), ()))
NN = (((1,), (0,)), ((), ()))
TILE = 512


def kernel(
    nx,
    nz,
    len_ref,
    pkv_ref,
    rkv_ref,
    routes_ref,
    gates_ref,
    q_hbm,
    g_hbm,
    tok_hbm,
    w_hbm,
    pout,
    rout,
    eout,
    q,
    g,
    tok,
    w,
    gath,
    num,
    prob,
    stat,
    low_a,
    low_g,
    part1,
    recv1,
    own_sum,
    part2,
    recv2,
    rows_out,
    rows_in,
    local_sem,
    zs,
    zr,
    xs,
    xr,
    es,
    er,
    cs,
    cr,
    s1,
    r1,
    s2,
    r2,
):
    seq = lax.axis_index("seq")
    me_e = lax.axis_index("expert")
    me_c = lax.axis_index("mp")
    me_x, me_z = seq // nz, seq % nz
    ne = rows_out.shape[0]
    cap = rows_out.shape[1]
    half = rows_out.shape[2]
    rows_all = q.shape[0]
    heads = rows_all // 128
    toks = gath.shape[3]
    blk = nz * toks

    def at_x(o):
        return {"seq": (me_x + o) % nx * nz + me_z}

    def at_z(o):
        return {"seq": me_x * nz + (me_z + o) % nz}

    def at_e(o):
        return {"expert": (me_e + o) % ne}

    sibling = {"mp": 1 - me_c}

    barrier = pltpu.get_barrier_semaphore()
    peers = [at_x(o) for o in range(1, nx)] + [at_z(o) for o in range(1, nz)]
    peers += [at_e(o) for o in range(1, ne)] + [sibling]
    for peer in peers:
        pl.semaphore_signal(barrier, inc=1, device_id=peer, device_id_type=MESH)

    tok_copy = pltpu.make_async_copy(
        tok_hbm.at[:, pl.ds(pl.multiple_of(me_c * half, half), half)], tok, local_sem.at[2]
    )
    tok_copy.start()
    for h in range(heads):
        cols = slice(h * HD, (h + 1) * HD)
        pltpu.make_async_copy(q_hbm.at[:, cols], q.at[h * 128 : (h + 1) * 128], local_sem.at[0]).start()
        pltpu.make_async_copy(g_hbm.at[:, cols], g.at[h * 128 : (h + 1) * 128], local_sem.at[1]).start()
    w_copy = pltpu.make_async_copy(w_hbm, w, local_sem.at[3])
    w_copy.start()
    gath[me_x, me_z] = pkv_ref[...]
    pl.semaphore_wait(barrier, len(peers))

    sends = []

    def remote(src, dst, send_sem, recv_sem, peer):
        copy = pltpu.make_async_remote_copy(
            src_ref=src,
            dst_ref=dst,
            send_sem=send_sem,
            recv_sem=recv_sem,
            device_id=peer,
            device_id_type=MESH,
        )
        copy.start()
        sends.append(copy)

    z_order = sorted(range(1, nz), key=lambda o: min(o, nz - o))
    own_block = gath.at[me_x, me_z]
    for o in reversed(z_order):
        remote(own_block, own_block, zs.at[o - 1], zr.at[me_z], at_z(o))

    def forward(k, zb):
        block = gath.at[me_x, zb]
        for o in range(1, nx):
            remote(block, block, xs.at[o - 1, k], xr.at[o - 1], at_x(o))

    forward(0, me_z)

    length = len_ref[0]
    lane = lax.broadcasted_iota(jnp.int32, (1, 128), 1)
    route_t = routes_ref[...].astype(F32).T
    gate_t = gates_ref[...].T
    valid = (lane < length).astype(F32)
    named, weight = [], []
    for e in range(ne):
        hit = route_t == float(e)
        named.append(jnp.max(hit.astype(F32), 0, keepdims=True))
        weight.append(jnp.sum(jnp.where(hit, gate_t, 0.0), 0, keepdims=True) * valid)
    named_all = jnp.concatenate(named, 0)
    upper = (
        lax.broadcasted_iota(jnp.int32, (128, 128), 0) <= lax.broadcasted_iota(jnp.int32, (128, 128), 1)
    ).astype(BF16)
    slot = lax.dot_general(named_all.astype(BF16), upper, NN, preferred_element_type=F32) - 1.0
    slot_id = lax.broadcasted_iota(jnp.int32, (cap, 128), 0).astype(F32)
    select, slot_gate = [], []
    for e in range(ne):
        chosen = jnp.where(slot[e : e + 1] == slot_id, named[e], 0.0)
        select.append(chosen)
        slot_gate.append(jnp.sum(chosen * weight[e], 1, keepdims=True))
    select = jnp.concatenate(select, 0).astype(BF16)
    slot_gate = jnp.concatenate(slot_gate, 0)
    tok_copy.wait()
    picked = lax.dot_general(select, tok[...], NN, preferred_element_type=F32)
    rows_out[...] = (picked * slot_gate).astype(BF16).reshape(ne, cap, half)

    for k, o in enumerate(z_order):
        zb = (me_z + o) % nz
        block = gath.at[me_x, zb]
        pltpu.make_async_copy(block, block, zr.at[zb]).wait()
        forward(k + 1, zb)

    for o in range(1, ne):
        there = (me_e + o) % ne
        remote(rows_out.at[there], rows_in.at[me_c, me_e], es.at[o - 1], er.at[me_e], at_e(o))
    rows_in[me_c, me_e] = rows_out[me_e]

    pltpu.make_async_copy(q, q, local_sem.at[0]).wait()
    pltpu.make_async_copy(g, g, local_sem.at[1]).wait()
    row_at = lax.broadcasted_iota(jnp.int32, (128, HD), 0)
    for h in range(heads):
        part = g[h * 128 : (h + 1) * 128, :]
        g[h * 128 : (h + 1) * 128, :] = jnp.where(row_at < length, part.astype(F32), 0.0).astype(BF16)

    def forward_block(b, keys, values, causal):
        n = keys.shape[0]
        for t in range(rows_all // TILE):
            rows = slice(t * TILE, (t + 1) * TILE)
            score = lax.dot_general(keys, q[rows, :], NT, preferred_element_type=F32)
            if causal:
                key_at = lax.broadcasted_iota(jnp.int32, (n, TILE), 0)
                query_at = lax.broadcasted_iota(jnp.int32, (n, TILE), 1) % 128
                score = jnp.where(key_at <= query_at, score, -jnp.inf)
            top = jnp.max(score, 0, keepdims=True)
            exps = jnp.exp2((score - top) * SCALE2)
            probs = lax.dot_general(values, g[rows, :], NT, preferred_element_type=F32)
            stat[0, b : b + 1, rows] = top
            stat[1, b : b + 1, rows] = jnp.sum(exps, 0, keepdims=True)
            stat[2, b : b + 1, rows] = jnp.sum(exps * probs, 0, keepdims=True)
            num[b, 0:n, rows] = exps
            prob[b, 0:n, rows] = probs

    own_b = nx
    forward_block(own_b, rkv_ref[0], rkv_ref[1], True)
    x_order = sorted(range(1, nx), key=lambda o: min(o, nx - o))
    for b, o in enumerate([0] + x_order):
        xb = (me_x + nx - o) % nx
        if o:
            came = gath.at[xb]
            pltpu.make_async_copy(came, came, xr.at[o - 1]).wait()
        forward_block(
            b, gath[xb, :, 0].reshape(blk, HD), gath[xb, :, 1].reshape(blk, HD), False
        )

    nb = nx + 1
    top = stat[0, 0:nb, :]
    factor = jnp.exp2((top - jnp.max(top, 0, keepdims=True)) * SCALE2)
    inverse = 1.0 / jnp.sum(stat[1, 0:nb, :] * factor, 0, keepdims=True)
    delta = jnp.sum(stat[2, 0:nb, :] * factor, 0, keepdims=True) * inverse
    stat[0, 0:nb, :] = factor * inverse
    stat[1, 0:1, :] = delta

    def backward_block(b, part, n):
        keys = slice(part * n, (part + 1) * n)
        for t in range(rows_all // 256):
            rows = slice(t * 256, (t + 1) * 256)
            attention = num[b, keys, rows] * stat[0, b : b + 1, rows]
            grad = attention * ((prob[b, keys, rows] - stat[1, 0:1, rows]) * SCALE)
            low_a[part, 0:n, rows] = attention.astype(BF16)
            low_g[part, 0:n, rows] = grad.astype(BF16)
        grad_v = lax.dot_general(low_a[part, 0:n, :], g[...], NN, preferred_element_type=F32)
        grad_k = lax.dot_general(low_g[part, 0:n, :], q[...], NN, preferred_element_type=F32)
        return grad_k, grad_v

    sub = min(128, blk)
    for b, o in reversed(list(enumerate([0] + x_order))):
        for part in range(blk // sub):
            grad_k, grad_v = backward_block(b, part, sub)
            keys = slice(part * sub, (part + 1) * sub)
            if o:
                part1[b - 1, 0, keys, :] = grad_k.astype(BF16)
                part1[b - 1, 1, keys, :] = grad_v.astype(BF16)
            else:
                own_sum[0, keys, :] = grad_k
                own_sum[1, keys, :] = grad_v
        if o:
            back = nx - o
            remote(part1.at[b - 1], recv1.at[o - 1], s1.at[o - 1], r1.at[o - 1], at_x(back))

    for o in range(1, nx):
        pltpu.make_async_copy(recv1.at[o - 1], recv1.at[o - 1], r1.at[o - 1]).wait()
    for zb in range(nz):
        keys = slice(zb * toks, (zb + 1) * toks)
        for kv in range(2):
            total = own_sum[kv, keys, :]
            for o in range(1, nx):
                total = total + recv1[o - 1, kv, keys, :].astype(F32)
            own_sum[kv, keys, :] = total
            part2[zb, kv] = total.astype(BF16)
    for o in reversed(z_order):
        zb = (me_z + o) % nz
        remote(part2.at[zb], recv2.at[me_z], s2.at[o - 1], r2.at[me_z], at_z(o))

    for o in range(1, ne):
        there = (me_e + o) % ne
        came = rows_in.at[me_c, there]
        pltpu.make_async_copy(came, came, er.at[there]).wait()
    remote(rows_in.at[me_c], rows_in.at[me_c], cs.at[0], cr.at[0], sibling)

    grad_k, grad_v = backward_block(own_b, 0, 128)
    rout[0] = grad_k
    rout[1] = grad_v

    w_copy.wait()
    other = rows_in.at[1 - me_c]
    pltpu.make_async_copy(other, other, cr.at[0]).wait()
    hidden = lax.dot_general(
        rows_in[0].reshape(ne * cap, half), w[:, 0:half], NT, preferred_element_type=F32
    )
    hidden = hidden + lax.dot_general(
        rows_in[1].reshape(ne * cap, half), w[:, half : 2 * half], NT, preferred_element_type=F32
    )
    eout[...] = hidden.astype(BF16).reshape(eout.shape)

    mine = pl.ds(pl.multiple_of(me_z * toks, toks), toks)
    total_k, total_v = own_sum[0, mine, :], own_sum[1, mine, :]
    for o in z_order:
        zb = (me_z + o) % nz
        came = recv2.at[zb]
        pltpu.make_async_copy(came, came, r2.at[zb]).wait()
        total_k = total_k + recv2[zb, 0].astype(F32)
        total_v = total_v + recv2[zb, 1].astype(F32)
    pout[0] = total_k
    pout[1] = total_v
    for copy in sends:
        copy.wait_send()


def local(nx, queries, out_grad, prompt_kv, resp_kv, lengths, grads, routes, gates, down_weight):
    ne = lax.axis_size("expert")
    toks = prompt_kv.shape[1]
    rows = queries.shape[2]
    width = queries.shape[3]
    heads = width // HD
    nz = lax.axis_size("seq") // nx
    features = grads.shape[3]
    half = features // 2
    hidden = down_weight.shape[1]
    cap = rows // 8
    blk = nz * toks
    vmem = pl.BlockSpec(memory_space=pltpu.VMEM)
    hbm = pl.BlockSpec(memory_space=pl.ANY)
    dma = pltpu.SemaphoreType.DMA
    out = pl.pallas_call(
        functools.partial(kernel, nx, nz),
        out_shape=[
            jax.ShapeDtypeStruct((2, toks, HD), F32),
            jax.ShapeDtypeStruct((2, rows, HD), F32),
            jax.ShapeDtypeStruct((ne, cap, hidden), BF16),
        ],
        in_specs=[pl.BlockSpec(memory_space=pltpu.SMEM)] + [vmem] * 4 + [hbm] * 4,
        out_specs=[vmem] * 3,
        scratch_shapes=[
            pltpu.VMEM((heads * rows, HD), BF16),
            pltpu.VMEM((heads * rows, HD), BF16),
            pltpu.VMEM((rows, half), BF16),
            pltpu.VMEM((hidden, features), BF16),
            pltpu.VMEM((nx, nz, 2, toks, HD), BF16),
            pltpu.VMEM((nx + 1, max(blk, rows), heads * rows), F32),
            pltpu.VMEM((nx + 1, max(blk, rows), heads * rows), F32),
            pltpu.VMEM((3, 8, heads * rows), F32),
            pltpu.VMEM((2, 128, heads * rows), BF16),
            pltpu.VMEM((2, 128, heads * rows), BF16),
            pltpu.VMEM((nx - 1, 2, blk, HD), BF16),
            pltpu.VMEM((nx - 1, 2, blk, HD), BF16),
            pltpu.VMEM((2, blk, HD), F32),
            pltpu.VMEM((nz, 2, toks, HD), BF16),
            pltpu.VMEM((nz, 2, toks, HD), BF16),
            pltpu.VMEM((ne, cap, half), BF16),
            pltpu.VMEM((2, ne, cap, half), BF16),
            dma((4,)),
            dma((nz - 1,)),
            dma((nz,)),
            dma((nx - 1, nz)),
            dma((nx - 1,)),
            dma((ne - 1,)),
            dma((ne,)),
            dma((1,)),
            dma((1,)),
            dma((nx - 1,)),
            dma((nx - 1,)),
            dma((nz - 1,)),
            dma((nz,)),
        ],
        compiler_params=pltpu.CompilerParams(
            collective_id=0, has_side_effects=True, vmem_limit_bytes=60 << 20
        ),
        name="moe_attention_backward",
    )(
        lengths[0],
        prompt_kv[0].transpose(1, 0, 2),
        resp_kv[0, 0].transpose(1, 0, 2),
        routes[0, 0],
        gates[0, 0],
        queries[0, 0],
        out_grad[0, 0],
        grads[0, 0],
        down_weight[0],
    )
    return (
        out[0].transpose(1, 0, 2)[None],
        out[1].transpose(1, 0, 2)[None, None],
        out[2][None, :, None],
    )


def solution(mesh):
    nx = 4 if mesh.shape["seq"] == 32 else 2
    placed = (
        P("expert", "seq", None, "mp"),
        P("expert", "seq", None, "mp"),
        P("expert", "seq", None, "mp"),
        P("expert", "seq", None, None, "mp"),
        P("expert", "seq"),
        P("expert", "seq", None, None),
        P("expert", "seq", None, None),
        P("expert", "seq", None, None),
        P("expert", "mp", None),
    )
    return jax.shard_map(
        functools.partial(local, nx),
        mesh=mesh,
        in_specs=placed,
        out_specs=(
            P("expert", "seq", None, "mp"),
            P("expert", "seq", None, None, "mp"),
            P("seq", None, "expert", None, "mp"),
        ),
        check_vma=False,
    )
```

time: 432 us -> 68.1 us (0.16)
  the two profiles are of different devices: /device:TPU:16 before, /device:TPU:6 now
where the time goes in v1:
time: 68.1 us; the launch traced here: 67.6 us
  Pallas kernels  56 us (82%)
  local copies, waits for them, and re-layouts  10.3 us (15%)
  between operations  1.29 us (2%)
    pallas_call x1, Pallas kernels, local(): pl.pallas_call(functools.partial(kernel, nx, nz), out_shape=[jax.ShapeDty...  56 us
    unnamed x7, local copies, waits for them, and re-layouts  10.3 us

profile of v1, /device:TPU:6, one launch (start us, length us, event | category | flops | bytes accessed | tf_op | source)
XLA Modules:
  0.0 67.6 jit_solution(17987554504153477879)
XLA Ops:
  1.3 1.3 %copy.22 = bf16[1,32,2,128]{3,1,2,0:T(8,128)(2,1)} copy(bf16[1,32,2,128]{3,2,1,0:T(2,128)(2,1)} %param.11) | data formatting | bytes 32768 | tf_op args[2]
  2.6 1.5 %copy.21 = bf16[1,1,128,2,128]{4,2,3,1,0:T(8,128)(2,1)} copy(bf16[1,1,128,2,128]{4,3,2,1,0:T(2,128)(2,1)} %param.12) | data formatting | bytes 131072 | tf_op args[3]
  4.1 1.4 %copy.14 = s32[1,1,128,8]{3,2,1,0:T(8,128)} copy(s32[1,1,128,8]{2,3,1,0:T(8,128)} %param.15) | data formatting | bytes 8192 | tf_op args[6]
  5.5 1.4 %copy.15 = f32[1,1,128,8]{3,2,1,0:T(8,128)} copy(f32[1,1,128,8]{2,3,1,0:T(8,128)} %param.16) | data formatting | bytes 8192 | tf_op args[7]
  6.9 56.0 %moe_attention_backward.1 = (f32[2,32,128]{2,1,0:T(8,128)}, f32[2,128,128]{2,1,0:T(8,128)}, bf16[8,16,768]{2,1,0:T(8,128)(2,1)}) custom-call(s32[1]{0:T(128)} %bitcast.26.len_ref, bf16[2,32,128]{2,1,0:T(8,128)(2,1)} %bitcast.36, bf16[2,128,128]{2,1,0:T(8,128)(2,1)} %bitcast.31, s32[128,8]{1,0:T(8,128)} %bitcast.32, f32[128,8]{1,0:T(8,128)} %bitcast.33, ...), custom_call_target="tpu_custom_call" | custom-call | tf_op jit(solution)/shard_map/moe_attention_backward/pallas_call | solution.py:310
  62.9 1.4 %copy.16 = f32[1,32,2,128]{3,2,1,0:T(2,128)} copy(f32[1,32,2,128]{3,1,2,0:T(8,128)} %bitcast.37) | data formatting | bytes 65536
  64.3 1.7 %copy.17 = f32[1,1,128,2,128]{4,3,2,1,0:T(2,128)} copy(f32[1,1,128,2,128]{4,2,3,1,0:T(8,128)} %bitcast.35) | data formatting | bytes 262144
  66.0 1.6 %copy.25 = bf16[1,8,1,16,768]{4,3,2,1,0:T(8,128)(2,1)} copy(bf16[1,8,1,16,768]{4,3,2,1,0:T(8,128)(2,1)} %bitcast.34) | data formatting | bytes 393216

commit v2 on v1

--- a/solution.py
+++ b/solution.py
@@ -51,6 +51,9 @@
     recv2,
     rows_out,
     rows_in,
+    own_grad,
+    own_prompt,
+    hid,
     local_sem,
     zs,
     zr,
@@ -104,7 +107,8 @@
         pltpu.make_async_copy(g_hbm.at[:, cols], g.at[h * 128 : (h + 1) * 128], local_sem.at[1]).start()
     w_copy = pltpu.make_async_copy(w_hbm, w, local_sem.at[3])
     w_copy.start()
-    gath[me_x, me_z] = pkv_ref[...]
+    gath[me_x, me_z, 0] = pkv_ref[:, 0, :]
+    gath[me_x, me_z, 1] = pkv_ref[:, 1, :]
     pl.semaphore_wait(barrier, len(peers))
 
     sends = []
@@ -133,10 +137,10 @@
 
     forward(0, me_z)
 
-    length = len_ref[0]
+    length = len_ref[0, 0]
     lane = lax.broadcasted_iota(jnp.int32, (1, 128), 1)
-    route_t = routes_ref[...].astype(F32).T
-    gate_t = gates_ref[...].T
+    route_t = routes_ref[...].astype(F32)
+    gate_t = gates_ref[...]
     valid = (lane < length).astype(F32)
     named, weight = [], []
     for e in range(ne):
@@ -160,17 +164,6 @@
     picked = lax.dot_general(select, tok[...], NN, preferred_element_type=F32)
     rows_out[...] = (picked * slot_gate).astype(BF16).reshape(ne, cap, half)
 
-    for k, o in enumerate(z_order):
-        zb = (me_z + o) % nz
-        block = gath.at[me_x, zb]
-        pltpu.make_async_copy(block, block, zr.at[zb]).wait()
-        forward(k + 1, zb)
-
-    for o in range(1, ne):
-        there = (me_e + o) % ne
-        remote(rows_out.at[there], rows_in.at[me_c, me_e], es.at[o - 1], er.at[me_e], at_e(o))
-    rows_in[me_c, me_e] = rows_out[me_e]
-
     pltpu.make_async_copy(q, q, local_sem.at[0]).wait()
     pltpu.make_async_copy(g, g, local_sem.at[1]).wait()
     row_at = lax.broadcasted_iota(jnp.int32, (128, HD), 0)
@@ -197,7 +190,19 @@
             prob[b, 0:n, rows] = probs
 
     own_b = nx
-    forward_block(own_b, rkv_ref[0], rkv_ref[1], True)
+    forward_block(own_b, rkv_ref[:, 0, :], rkv_ref[:, 1, :], True)
+
+    for k, o in enumerate(z_order):
+        zb = (me_z + o) % nz
+        block = gath.at[me_x, zb]
+        pltpu.make_async_copy(block, block, zr.at[zb]).wait()
+        forward(k + 1, zb)
+
+    for o in range(1, ne):
+        there = (me_e + o) % ne
+        remote(rows_out.at[there], rows_in.at[me_c, me_e], es.at[o - 1], er.at[me_e], at_e(o))
+    rows_in[me_c, me_e] = rows_out[me_e]
+
     x_order = sorted(range(1, nx), key=lambda o: min(o, nx - o))
     for b, o in enumerate([0] + x_order):
         xb = (me_x + nx - o) % nx
@@ -216,46 +221,66 @@
     stat[0, 0:nb, :] = factor * inverse
     stat[1, 0:1, :] = delta
 
-    def backward_block(b, part, n):
-        keys = slice(part * n, (part + 1) * n)
+    def backward_block(b, keys, n):
         for t in range(rows_all // 256):
             rows = slice(t * 256, (t + 1) * 256)
             attention = num[b, keys, rows] * stat[0, b : b + 1, rows]
             grad = attention * ((prob[b, keys, rows] - stat[1, 0:1, rows]) * SCALE)
-            low_a[part, 0:n, rows] = attention.astype(BF16)
-            low_g[part, 0:n, rows] = grad.astype(BF16)
-        grad_v = lax.dot_general(low_a[part, 0:n, :], g[...], NN, preferred_element_type=F32)
-        grad_k = lax.dot_general(low_g[part, 0:n, :], q[...], NN, preferred_element_type=F32)
+            low_a[0:n, rows] = attention.astype(BF16)
+            low_g[0:n, rows] = grad.astype(BF16)
+        grad_v = lax.dot_general(low_a[0:n, :], g[...], NN, preferred_element_type=F32)
+        grad_k = lax.dot_general(low_g[0:n, :], q[...], NN, preferred_element_type=F32)
         return grad_k, grad_v
 
-    sub = min(128, blk)
-    for b, o in reversed(list(enumerate([0] + x_order))):
-        for part in range(blk // sub):
-            grad_k, grad_v = backward_block(b, part, sub)
-            keys = slice(part * sub, (part + 1) * sub)
+    hz = nz // 2
+    sub = hz * toks
+    my_half, my_at = me_z // hz, me_z % hz
+    halves = [1 - my_half, my_half]
+    for step in range(2):
+        keys = pl.ds(pl.multiple_of(halves[step] * sub, sub), sub)
+        for b, o in reversed(list(enumerate([0] + x_order))):
+            grad_k, grad_v = backward_block(b, keys, sub)
             if o:
-                part1[b - 1, 0, keys, :] = grad_k.astype(BF16)
-                part1[b - 1, 1, keys, :] = grad_v.astype(BF16)
+                part1[b - 1, step, 0] = grad_k.astype(BF16)
+                part1[b - 1, step, 1] = grad_v.astype(BF16)
+                remote(
+                    part1.at[b - 1, step],
+                    recv1.at[o - 1, step],
+                    s1.at[o - 1, step],
+                    r1.at[o - 1, step],
+                    at_x(nx - o),
+                )
             else:
-                own_sum[0, keys, :] = grad_k
-                own_sum[1, keys, :] = grad_v
-        if o:
-            back = nx - o
-            remote(part1.at[b - 1], recv1.at[o - 1], s1.at[o - 1], r1.at[o - 1], at_x(back))
-
-    for o in range(1, nx):
-        pltpu.make_async_copy(recv1.at[o - 1], recv1.at[o - 1], r1.at[o - 1]).wait()
-    for zb in range(nz):
-        keys = slice(zb * toks, (zb + 1) * toks)
-        for kv in range(2):
-            total = own_sum[kv, keys, :]
-            for o in range(1, nx):
-                total = total + recv1[o - 1, kv, keys, :].astype(F32)
-            own_sum[kv, keys, :] = total
-            part2[zb, kv] = total.astype(BF16)
-    for o in reversed(z_order):
-        zb = (me_z + o) % nz
-        remote(part2.at[zb], recv2.at[me_z], s2.at[o - 1], r2.at[me_z], at_z(o))
+                own_sum[step, 0] = grad_k
+                own_sum[step, 1] = grad_v
+
+    grad_k, grad_v = backward_block(own_b, slice(0, 128), 128)
+    own_grad[0] = grad_k
+    own_grad[1] = grad_v
+    own_out = pltpu.make_async_copy(own_grad, rout, local_sem.at[4])
+    own_out.start()
+
+    for step in range(2):
+        for o in range(1, nx):
+            came = recv1.at[o - 1, step]
+            pltpu.make_async_copy(came, came, r1.at[o - 1, step]).wait()
+        for j in range(hz):
+            keys = slice(j * toks, (j + 1) * toks)
+            for kv in range(2):
+                total = own_sum[step, kv, keys, :]
+                for o in range(1, nx):
+                    total = total + recv1[o - 1, step, kv, keys, :].astype(F32)
+                own_sum[step, kv, keys, :] = total
+                part2[step, j, kv] = total.astype(BF16)
+        for o in range(step, hz):
+            j = (my_at + o) % hz
+            remote(
+                part2.at[step, j],
+                recv2.at[me_z],
+                s2.at[step * hz + o],
+                r2.at[me_z],
+                {"seq": me_x * nz + halves[step] * hz + j},
+            )
 
     for o in range(1, ne):
         there = (me_e + o) % ne
@@ -263,10 +288,6 @@
         pltpu.make_async_copy(came, came, er.at[there]).wait()
     remote(rows_in.at[me_c], rows_in.at[me_c], cs.at[0], cr.at[0], sibling)
 
-    grad_k, grad_v = backward_block(own_b, 0, 128)
-    rout[0] = grad_k
-    rout[1] = grad_v
-
     w_copy.wait()
     other = rows_in.at[1 - me_c]
     pltpu.make_async_copy(other, other, cr.at[0]).wait()
@@ -276,20 +297,41 @@
     hidden = hidden + lax.dot_general(
         rows_in[1].reshape(ne * cap, half), w[:, half : 2 * half], NT, preferred_element_type=F32
     )
-    eout[...] = hidden.astype(BF16).reshape(eout.shape)
-
-    mine = pl.ds(pl.multiple_of(me_z * toks, toks), toks)
-    total_k, total_v = own_sum[0, mine, :], own_sum[1, mine, :]
+    hid[...] = hidden.astype(BF16).reshape(hid.shape)
+    hid_out = pltpu.make_async_copy(hid, eout, local_sem.at[5])
+    hid_out.start()
+
+    mine = pl.ds(pl.multiple_of(my_at * toks, toks), toks)
+    total_k, total_v = own_sum[1, 0, mine, :], own_sum[1, 1, mine, :]
     for o in z_order:
         zb = (me_z + o) % nz
         came = recv2.at[zb]
         pltpu.make_async_copy(came, came, r2.at[zb]).wait()
         total_k = total_k + recv2[zb, 0].astype(F32)
         total_v = total_v + recv2[zb, 1].astype(F32)
-    pout[0] = total_k
-    pout[1] = total_v
+    own_prompt[0] = total_k
+    own_prompt[1] = total_v
+    prompt_out = pltpu.make_async_copy(own_prompt, pout, local_sem.at[6])
+    prompt_out.start()
+    own_out.wait()
+    hid_out.wait()
+    prompt_out.wait()
     for copy in sends:
         copy.wait_send()
+
+
+def place(pin, rin, ein, pout, rout, eout, sem):
+    copies = [
+        pltpu.make_async_copy(pin.at[0], pout.at[:, 0, :], sem.at[0]),
+        pltpu.make_async_copy(pin.at[1], pout.at[:, 1, :], sem.at[1]),
+        pltpu.make_async_copy(rin.at[0], rout.at[:, 0, :], sem.at[2]),
+        pltpu.make_async_copy(rin.at[1], rout.at[:, 1, :], sem.at[3]),
+        pltpu.make_async_copy(ein, eout, sem.at[4]),
+    ]
+    for copy in copies:
+        copy.start()
+    for copy in copies:
+        copy.wait()
 
 
 def local(nx, queries, out_grad, prompt_kv, resp_kv, lengths, grads, routes, gates, down_weight):
@@ -315,7 +357,7 @@
             jax.ShapeDtypeStruct((ne, cap, hidden), BF16),
         ],
         in_specs=[pl.BlockSpec(memory_space=pltpu.SMEM)] + [vmem] * 4 + [hbm] * 4,
-        out_specs=[vmem] * 3,
+        out_specs=[hbm] * 3,
         scratch_shapes=[
             pltpu.VMEM((heads * rows, HD), BF16),
             pltpu.VMEM((heads * rows, HD), BF16),
@@ -325,16 +367,19 @@
             pltpu.VMEM((nx + 1, max(blk, rows), heads * rows), F32),
             pltpu.VMEM((nx + 1, max(blk, rows), heads * rows), F32),
             pltpu.VMEM((3, 8, heads * rows), F32),
-            pltpu.VMEM((2, 128, heads * rows), BF16),
-            pltpu.VMEM((2, 128, heads * rows), BF16),
-            pltpu.VMEM((nx - 1, 2, blk, HD), BF16),
-            pltpu.VMEM((nx - 1, 2, blk, HD), BF16),
-            pltpu.VMEM((2, blk, HD), F32),
-            pltpu.VMEM((nz, 2, toks, HD), BF16),
+            pltpu.VMEM((128, heads * rows), BF16),
+            pltpu.VMEM((128, heads * rows), BF16),
+            pltpu.VMEM((nx - 1, 2, 2, blk // 2, HD), BF16),
+            pltpu.VMEM((nx - 1, 2, 2, blk // 2, HD), BF16),
+            pltpu.VMEM((2, 2, blk // 2, HD), F32),
+            pltpu.VMEM((2, nz // 2, 2, toks, HD), BF16),
             pltpu.VMEM((nz, 2, toks, HD), BF16),
             pltpu.VMEM((ne, cap, half), BF16),
             pltpu.VMEM((2, ne, cap, half), BF16),
-            dma((4,)),
+            pltpu.VMEM((2, rows, HD), F32),
+            pltpu.VMEM((2, toks, HD), F32),
+            pltpu.VMEM((ne, cap, hidden), BF16),
+            dma((7,)),
             dma((nz - 1,)),
             dma((nz,)),
             dma((nx - 1, nz)),
@@ -343,9 +388,9 @@
             dma((ne,)),
             dma((1,)),
             dma((1,)),
-            dma((nx - 1,)),
-            dma((nx - 1,)),
-            dma((nz - 1,)),
+            dma((nx - 1, 2)),
+            dma((nx - 1, 2)),
+            dma((nz,)),
             dma((nz,)),
         ],
         compiler_params=pltpu.CompilerParams(
@@ -353,21 +398,30 @@
         ),
         name="moe_attention_backward",
     )(
-        lengths[0],
-        prompt_kv[0].transpose(1, 0, 2),
-        resp_kv[0, 0].transpose(1, 0, 2),
-        routes[0, 0],
-        gates[0, 0],
+        lengths,
+        prompt_kv[0],
+        resp_kv[0, 0],
+        routes[0, 0].T,
+        gates[0, 0].T,
         queries[0, 0],
         out_grad[0, 0],
         grads[0, 0],
         down_weight[0],
     )
-    return (
-        out[0].transpose(1, 0, 2)[None],
-        out[1].transpose(1, 0, 2)[None, None],
-        out[2][None, :, None],
-    )
+    placed = pl.pallas_call(
+        place,
+        out_shape=[
+            jax.ShapeDtypeStruct((toks, 2, HD), F32),
+            jax.ShapeDtypeStruct((rows, 2, HD), F32),
+            jax.ShapeDtypeStruct((ne, cap, hidden), BF16),
+        ],
+        in_specs=[hbm] * 3,
+        out_specs=[hbm] * 3,
+        scratch_shapes=[dma((5,))],
+        compiler_params=pltpu.CompilerParams(vmem_limit_bytes=60 << 20),
+        name="place_outputs",
+    )(*out)
+    return (placed[0][None], placed[1][None, None], placed[2][None, :, None])
 
 
 def solution(mesh):

time: 68.1 us -> 68.7 us (level)
  Pallas kernels: 56 us -> 67.3 us
  local copies, waits for them, and re-layouts: 10.3 us -> 0 us
    pallas_call x0 -> x1, Pallas kernels: none -> 12.1 us  [local(): pl.pallas_call(place, out_shape=[jax.ShapeDtypeStruct((toks, 2, HD), F32)...]
    unnamed x7 -> x0, local copies, waits for them, and re-layouts: 10.3 us -> none
    pallas_call x1, Pallas kernels: 56 us -> 55.2 us  [local(): pl.pallas_call(functools.partial(kernel, nx, nz), out_shape=[jax.ShapeDty...]
where the time goes in v2:
time: 68.7 us; the launch traced here: 68.6 us
  Pallas kernels  67.3 us (98%)
  between operations  1.29 us (2%)
    pallas_call x1, Pallas kernels, local(): pl.pallas_call(functools.partial(kernel, nx, nz), out_shape=[jax.ShapeDty...  55.2 us
    pallas_call x1, Pallas kernels, local(): pl.pallas_call(place, out_shape=[jax.ShapeDtypeStruct((toks, 2, HD), F32)...  12.1 us

profile of v2, /device:TPU:6, one launch (start us, length us, event | category | flops | bytes accessed | tf_op | source)
XLA Modules:
  0.0 68.6 jit_solution(332225171987506767)
XLA Ops:
  1.3 55.2 %moe_attention_backward.1 = (f32[2,32,128]{2,1,0:T(8,128)}, f32[2,128,128]{2,1,0:T(8,128)}, bf16[8,16,768]{2,1,0:T(8,128)(2,1)}) custom-call(s32[1,1]{1,0:T(1,128)S(6)} %copy.13.len_ref, bf16[32,2,128]{2,1,0:T(2,128)(2,1)} %bitcast.22, bf16[128,2,128]{2,1,0:T(2,128)(2,1)} %bitcast.21, s32[8,128]{1,0:T(8,128)} %bitcast.23, f32[8,128]{1,0:T(8,128)} %bitcast.24, ...), custom_call_target="tpu_custom_call" | custom-call | tf_op jit(solution)/shard_map/moe_attention_backward/pallas_call | solution.py:352
  56.5 12.1 %place_outputs.1 = (f32[32,2,128]{2,1,0:T(2,128)}, f32[128,2,128]{2,1,0:T(2,128)}, bf16[8,16,768]{2,1,0:T(8,128)(2,1)}) custom-call(f32[2,32,128]{2,1,0:T(8,128)} %get-tuple-element.9.pin, f32[2,128,128]{2,1,0:T(8,128)} %get-tuple-element.10.rin, bf16[8,16,768]{2,1,0:T(8,128)(2,1)} %get-tuple-element.11.ein), custom_call_target="tpu_custom_call" | custom-call | tf_op jit(solution)/shard_map/place_outputs/pallas_call | solution.py:411

commit v3 on v2

--- a/solution.py
+++ b/solution.py
@@ -67,6 +67,7 @@
     r1,
     s2,
     r2,
+    ready,
 ):
     seq = lax.axis_index("seq")
     me_e = lax.axis_index("expert")
@@ -86,14 +87,26 @@
     def at_z(o):
         return {"seq": me_x * nz + (me_z + o) % nz}
 
-    def at_e(o):
-        return {"expert": (me_e + o) % ne}
+    ny = ne // 2
+    me_h, me_y = me_e // ny, me_e % ny
+
+    def at_y(o):
+        return me_h * ny + (me_y + o) % ny
+
+    def far(o):
+        return (1 - me_h) * ny + (me_y + o) % ny
 
     sibling = {"mp": 1 - me_c}
 
     barrier = pltpu.get_barrier_semaphore()
     peers = [at_x(o) for o in range(1, nx)] + [at_z(o) for o in range(1, nz)]
-    peers += [at_e(o) for o in range(1, ne)] + [sibling]
+    peers += [{"expert": at_y(o)} for o in range(1, ny)] + [sibling]
+
+    @pl.when(me_h == 0)
+    def _():
+        for o in range(ny):
+            pl.semaphore_signal(barrier, inc=1, device_id={"expert": far(o)}, device_id_type=MESH)
+
     for peer in peers:
         pl.semaphore_signal(barrier, inc=1, device_id=peer, device_id_type=MESH)
 
@@ -109,7 +122,13 @@
     w_copy.start()
     gath[me_x, me_z, 0] = pkv_ref[:, 0, :]
     gath[me_x, me_z, 1] = pkv_ref[:, 1, :]
-    pl.semaphore_wait(barrier, len(peers))
+    pl.semaphore_wait(barrier, len(peers) + me_h * ny)
+
+    @pl.when(me_h == 1)
+    def _():
+        for o in range(ny):
+            pl.semaphore_signal(ready, inc=1, device_id={"expert": far(o)}, device_id_type=MESH)
+
 
     sends = []
 
@@ -198,9 +217,26 @@
         pltpu.make_async_copy(block, block, zr.at[zb]).wait()
         forward(k + 1, zb)
 
-    for o in range(1, ne):
-        there = (me_e + o) % ne
-        remote(rows_out.at[there], rows_in.at[me_c, me_e], es.at[o - 1], er.at[me_e], at_e(o))
+    def routed(there, k):
+        return pltpu.make_async_remote_copy(
+            src_ref=rows_out.at[there],
+            dst_ref=rows_in.at[me_c, me_e],
+            send_sem=es.at[k],
+            recv_sem=er.at[me_e],
+            device_id={"expert": there},
+            device_id_type=MESH,
+        )
+
+    near_rows = [routed(at_y(o), o - 1) for o in range(1, ny)]
+    far_rows = [routed(far(o), ny - 1 + o) for o in range(ny)]
+
+    @pl.when(me_h == 1)
+    def _():
+        for copy in far_rows:
+            copy.start()
+
+    for copy in near_rows:
+        copy.start()
     rows_in[me_c, me_e] = rows_out[me_e]
 
     x_order = sorted(range(1, nx), key=lambda o: min(o, nx - o))
@@ -220,6 +256,12 @@
     delta = jnp.sum(stat[2, 0:nb, :] * factor, 0, keepdims=True) * inverse
     stat[0, 0:nb, :] = factor * inverse
     stat[1, 0:1, :] = delta
+
+    @pl.when(me_h == 0)
+    def _():
+        pl.semaphore_wait(ready, ny)
+        for copy in far_rows:
+            copy.start()
 
     def backward_block(b, keys, n):
         for t in range(rows_all // 256):
@@ -316,22 +358,15 @@
     own_out.wait()
     hid_out.wait()
     prompt_out.wait()
-    for copy in sends:
+    for copy in sends + near_rows + far_rows:
         copy.wait_send()
 
 
-def place(pin, rin, ein, pout, rout, eout, sem):
-    copies = [
-        pltpu.make_async_copy(pin.at[0], pout.at[:, 0, :], sem.at[0]),
-        pltpu.make_async_copy(pin.at[1], pout.at[:, 1, :], sem.at[1]),
-        pltpu.make_async_copy(rin.at[0], rout.at[:, 0, :], sem.at[2]),
-        pltpu.make_async_copy(rin.at[1], rout.at[:, 1, :], sem.at[3]),
-        pltpu.make_async_copy(ein, eout, sem.at[4]),
-    ]
-    for copy in copies:
-        copy.start()
-    for copy in copies:
-        copy.wait()
+def place(pin, rin, ein, pout, rout, eout):
+    for kv in range(2):
+        pout[:, kv, :] = pin[kv]
+        rout[:, kv, :] = rin[kv]
+    eout[...] = ein[...]
 
 
 def local(nx, queries, out_grad, prompt_kv, resp_kv, lengths, grads, routes, gates, down_weight):
@@ -392,6 +427,7 @@
             dma((nx - 1, 2)),
             dma((nz,)),
             dma((nz,)),
+            pltpu.SemaphoreType.REGULAR,
         ],
         compiler_params=pltpu.CompilerParams(
             collective_id=0, has_side_effects=True, vmem_limit_bytes=60 << 20
@@ -415,9 +451,8 @@
             jax.ShapeDtypeStruct((rows, 2, HD), F32),
             jax.ShapeDtypeStruct((ne, cap, hidden), BF16),
         ],
-        in_specs=[hbm] * 3,
-        out_specs=[hbm] * 3,
-        scratch_shapes=[dma((5,))],
+        in_specs=[vmem] * 3,
+        out_specs=[vmem] * 3,
         compiler_params=pltpu.CompilerParams(vmem_limit_bytes=60 << 20),
         name="place_outputs",
     )(*out)

time: 68.7 us -> 50.3 us (0.73)
  Pallas kernels: 67.3 us -> 48.4 us
    pallas_call x1, Pallas kernels: 12.1 us -> 1.82 us  [local(): pl.pallas_call(place, out_shape=[jax.ShapeDtypeStruct((toks, 2, HD), F32)...]
    pallas_call x1, Pallas kernels: 55.2 us -> 46.6 us  [local(): pl.pallas_call(functools.partial(kernel, nx, nz), out_shape=[jax.ShapeDty...]
where the time goes in v3:
time: 50.3 us; the launch traced here: 49.7 us
  Pallas kernels  48.4 us (96%)
  between operations  1.29 us (3%)
    pallas_call x1, Pallas kernels, local(): pl.pallas_call(functools.partial(kernel, nx, nz), out_shape=[jax.ShapeDty...  46.6 us
    pallas_call x1, Pallas kernels, local(): pl.pallas_call(place, out_shape=[jax.ShapeDtypeStruct((toks, 2, HD), F32)...  1.82 us

profile of v3, /device:TPU:6, one launch (start us, length us, event | category | flops | bytes accessed | tf_op | source)
XLA Modules:
  0.0 49.7 jit_solution(3298024691379051264)
XLA Ops:
  1.3 46.6 %moe_attention_backward.1 = (f32[2,32,128]{2,1,0:T(8,128)}, f32[2,128,128]{2,1,0:T(8,128)}, bf16[8,16,768]{2,1,0:T(8,128)(2,1)}) custom-call(s32[1,1]{1,0:T(1,128)S(6)} %copy.13.len_ref, bf16[32,2,128]{2,1,0:T(2,128)(2,1)} %bitcast.22, bf16[128,2,128]{2,1,0:T(2,128)(2,1)} %bitcast.21, s32[8,128]{1,0:T(8,128)} %bitcast.23, f32[8,128]{1,0:T(8,128)} %bitcast.24, ...), custom_call_target="tpu_custom_call" | custom-call | tf_op jit(solution)/shard_map/moe_attention_backward/pallas_call | solution.py:387
  47.8 1.8 %place_outputs.1 = (f32[32,2,128]{2,1,0:T(2,128)}, f32[128,2,128]{2,1,0:T(2,128)}, bf16[8,16,768]{2,1,0:T(8,128)(2,1)}) custom-call(f32[2,32,128]{2,1,0:T(8,128)} %get-tuple-element.9.pin, f32[2,128,128]{2,1,0:T(8,128)} %get-tuple-element.10.rin, bf16[8,16,768]{2,1,0:T(8,128)(2,1)} %get-tuple-element.11.ein), custom_call_target="tpu_custom_call" | custom-call | tf_op jit(solution)/shard_map/place_outputs/pallas_call | solution.py:447

commit v4 on v3

--- a/solution.py
+++ b/solution.py
@@ -23,10 +23,10 @@
     nx,
     nz,
     len_ref,
-    pkv_ref,
-    rkv_ref,
-    routes_ref,
-    gates_ref,
+    pkv_hbm,
+    rkv_hbm,
+    routes_hbm,
+    gates_hbm,
     q_hbm,
     g_hbm,
     tok_hbm,
@@ -54,6 +54,10 @@
     own_grad,
     own_prompt,
     hid,
+    pkv_ref,
+    rkv_ref,
+    routes_ref,
+    gates_ref,
     local_sem,
     zs,
     zr,
@@ -110,6 +114,14 @@
     for peer in peers:
         pl.semaphore_signal(barrier, inc=1, device_id=peer, device_id_type=MESH)
 
+    small = [
+        pltpu.make_async_copy(src, dst, local_sem.at[7 + k])
+        for k, (src, dst) in enumerate(
+            [(pkv_hbm, pkv_ref), (routes_hbm, routes_ref), (gates_hbm, gates_ref), (rkv_hbm, rkv_ref)]
+        )
+    ]
+    for copy in small:
+        copy.start()
     tok_copy = pltpu.make_async_copy(
         tok_hbm.at[:, pl.ds(pl.multiple_of(me_c * half, half), half)], tok, local_sem.at[2]
     )
@@ -120,6 +132,7 @@
         pltpu.make_async_copy(g_hbm.at[:, cols], g.at[h * 128 : (h + 1) * 128], local_sem.at[1]).start()
     w_copy = pltpu.make_async_copy(w_hbm, w, local_sem.at[3])
     w_copy.start()
+    small[0].wait()
     gath[me_x, me_z, 0] = pkv_ref[:, 0, :]
     gath[me_x, me_z, 1] = pkv_ref[:, 1, :]
     pl.semaphore_wait(barrier, len(peers) + me_h * ny)
@@ -158,6 +171,8 @@
 
     length = len_ref[0, 0]
     lane = lax.broadcasted_iota(jnp.int32, (1, 128), 1)
+    small[1].wait()
+    small[2].wait()
     route_t = routes_ref[...].astype(F32)
     gate_t = gates_ref[...]
     valid = (lane < length).astype(F32)
@@ -209,6 +224,7 @@
             prob[b, 0:n, rows] = probs
 
     own_b = nx
+    small[3].wait()
     forward_block(own_b, rkv_ref[:, 0, :], rkv_ref[:, 1, :], True)
 
     for k, o in enumerate(z_order):
@@ -248,6 +264,12 @@
         forward_block(
             b, gath[xb, :, 0].reshape(blk, HD), gath[xb, :, 1].reshape(blk, HD), False
         )
+        if b == 0:
+            @pl.when(me_h == 0)
+            def _():
+                pl.semaphore_wait(ready, ny)
+                for copy in far_rows:
+                    copy.start()
 
     nb = nx + 1
     top = stat[0, 0:nb, :]
@@ -257,21 +279,15 @@
     stat[0, 0:nb, :] = factor * inverse
     stat[1, 0:1, :] = delta
 
-    @pl.when(me_h == 0)
-    def _():
-        pl.semaphore_wait(ready, ny)
-        for copy in far_rows:
-            copy.start()
-
-    def backward_block(b, keys, n):
+    def backward_block(b, keys, n, at):
         for t in range(rows_all // 256):
             rows = slice(t * 256, (t + 1) * 256)
             attention = num[b, keys, rows] * stat[0, b : b + 1, rows]
             grad = attention * ((prob[b, keys, rows] - stat[1, 0:1, rows]) * SCALE)
-            low_a[0:n, rows] = attention.astype(BF16)
-            low_g[0:n, rows] = grad.astype(BF16)
-        grad_v = lax.dot_general(low_a[0:n, :], g[...], NN, preferred_element_type=F32)
-        grad_k = lax.dot_general(low_g[0:n, :], q[...], NN, preferred_element_type=F32)
+            low_a[at, 0:n, rows] = attention.astype(BF16)
+            low_g[at, 0:n, rows] = grad.astype(BF16)
+        grad_v = lax.dot_general(low_a[at, 0:n, :], g[...], NN, preferred_element_type=F32)
+        grad_k = lax.dot_general(low_g[at, 0:n, :], q[...], NN, preferred_element_type=F32)
         return grad_k, grad_v
 
     hz = nz // 2
@@ -281,7 +297,7 @@
     for step in range(2):
         keys = pl.ds(pl.multiple_of(halves[step] * sub, sub), sub)
         for b, o in reversed(list(enumerate([0] + x_order))):
-            grad_k, grad_v = backward_block(b, keys, sub)
+            grad_k, grad_v = backward_block(b, keys, sub, b % 2)
             if o:
                 part1[b - 1, step, 0] = grad_k.astype(BF16)
                 part1[b - 1, step, 1] = grad_v.astype(BF16)
@@ -296,7 +312,7 @@
                 own_sum[step, 0] = grad_k
                 own_sum[step, 1] = grad_v
 
-    grad_k, grad_v = backward_block(own_b, slice(0, 128), 128)
+    grad_k, grad_v = backward_block(own_b, slice(0, 128), 128, 1)
     own_grad[0] = grad_k
     own_grad[1] = grad_v
     own_out = pltpu.make_async_copy(own_grad, rout, local_sem.at[4])
@@ -391,7 +407,7 @@
             jax.ShapeDtypeStruct((2, rows, HD), F32),
             jax.ShapeDtypeStruct((ne, cap, hidden), BF16),
         ],
-        in_specs=[pl.BlockSpec(memory_space=pltpu.SMEM)] + [vmem] * 4 + [hbm] * 4,
+        in_specs=[pl.BlockSpec(memory_space=pltpu.SMEM)] + [hbm] * 8,
         out_specs=[hbm] * 3,
         scratch_shapes=[
             pltpu.VMEM((heads * rows, HD), BF16),
@@ -402,8 +418,8 @@
             pltpu.VMEM((nx + 1, max(blk, rows), heads * rows), F32),
             pltpu.VMEM((nx + 1, max(blk, rows), heads * rows), F32),
             pltpu.VMEM((3, 8, heads * rows), F32),
-            pltpu.VMEM((128, heads * rows), BF16),
-            pltpu.VMEM((128, heads * rows), BF16),
+            pltpu.VMEM((2, 128, heads * rows), BF16),
+            pltpu.VMEM((2, 128, heads * rows), BF16),
             pltpu.VMEM((nx - 1, 2, 2, blk // 2, HD), BF16),
             pltpu.VMEM((nx - 1, 2, 2, blk // 2, HD), BF16),
             pltpu.VMEM((2, 2, blk // 2, HD), F32),
@@ -414,7 +430,11 @@
             pltpu.VMEM((2, rows, HD), F32),
             pltpu.VMEM((2, toks, HD), F32),
             pltpu.VMEM((ne, cap, hidden), BF16),
-            dma((7,)),
+            pltpu.VMEM((toks, 2, HD), BF16),
+            pltpu.VMEM((rows, 2, HD), BF16),
+            pltpu.VMEM((routes.shape[3], rows), jnp.int32),
+            pltpu.VMEM((routes.shape[3], rows), F32),
+            dma((11,)),
             dma((nz - 1,)),
             dma((nz,)),
             dma((nx - 1, nz)),

time: 50.3 us -> 48.5 us (0.964)
  the two profiles are of different devices: /device:TPU:6 before, /device:TPU:1 now
where the time goes in v4:
time: 48.5 us; the launch traced here: 48.3 us
  Pallas kernels  47 us (97%)
  between operations  1.29 us (3%)
    pallas_call x1, Pallas kernels, local(): pl.pallas_call(functools.partial(kernel, nx, nz), out_shape=[jax.ShapeDty...  45.2 us
    pallas_call x1, Pallas kernels, local(): pl.pallas_call(place, out_shape=[jax.ShapeDtypeStruct((toks, 2, HD), F32)...  1.82 us

profile of v4, /device:TPU:1, one launch (start us, length us, event | category | flops | bytes accessed | tf_op | source)
XLA Modules:
  0.0 48.3 jit_solution(7690885607792376803)
XLA Ops:
  1.3 45.2 %moe_attention_backward.1 = (f32[2,32,128]{2,1,0:T(8,128)}, f32[2,128,128]{2,1,0:T(8,128)}, bf16[8,16,768]{2,1,0:T(8,128)(2,1)}) custom-call(s32[1,1]{1,0:T(1,128)S(6)} %copy.13.len_ref, bf16[32,2,128]{2,1,0:T(2,128)(2,1)} %bitcast.22, bf16[128,2,128]{2,1,0:T(2,128)(2,1)} %bitcast.21, s32[8,128]{1,0:T(8,128)} %bitcast.23, f32[8,128]{1,0:T(8,128)} %bitcast.24, ...), custom_call_target="tpu_custom_call" | custom-call | tf_op jit(solution)/shard_map/moe_attention_backward/pallas_call | solution.py:403
  46.5 1.8 %place_outputs.1 = (f32[32,2,128]{2,1,0:T(2,128)}, f32[128,2,128]{2,1,0:T(2,128)}, bf16[8,16,768]{2,1,0:T(8,128)(2,1)}) custom-call(f32[2,32,128]{2,1,0:T(8,128)} %get-tuple-element.9.pin, f32[2,128,128]{2,1,0:T(8,128)} %get-tuple-element.10.rin, bf16[8,16,768]{2,1,0:T(8,128)(2,1)} %get-tuple-element.11.ein), custom_call_target="tpu_custom_call" | custom-call | tf_op jit(solution)/shard_map/place_outputs/pallas_call | solution.py:467

commit v5 on v4

--- a/solution.py
+++ b/solution.py
@@ -198,6 +198,28 @@
     picked = lax.dot_general(select, tok[...], NN, preferred_element_type=F32)
     rows_out[...] = (picked * slot_gate).astype(BF16).reshape(ne, cap, half)
 
+    def routed(there, k):
+        return pltpu.make_async_remote_copy(
+            src_ref=rows_out.at[there],
+            dst_ref=rows_in.at[me_c, me_e],
+            send_sem=es.at[k],
+            recv_sem=er.at[me_e],
+            device_id={"expert": there},
+            device_id_type=MESH,
+        )
+
+    near_rows = [routed(at_y(o), o - 1) for o in range(1, ny)]
+    far_rows = [routed(far(o), ny - 1 + o) for o in range(ny)]
+
+    @pl.when(me_h == 1)
+    def _():
+        for copy in far_rows:
+            copy.start()
+
+    for copy in near_rows:
+        copy.start()
+    rows_in[me_c, me_e] = rows_out[me_e]
+
     pltpu.make_async_copy(q, q, local_sem.at[0]).wait()
     pltpu.make_async_copy(g, g, local_sem.at[1]).wait()
     row_at = lax.broadcasted_iota(jnp.int32, (128, HD), 0)
@@ -232,28 +254,6 @@
         block = gath.at[me_x, zb]
         pltpu.make_async_copy(block, block, zr.at[zb]).wait()
         forward(k + 1, zb)
-
-    def routed(there, k):
-        return pltpu.make_async_remote_copy(
-            src_ref=rows_out.at[there],
-            dst_ref=rows_in.at[me_c, me_e],
-            send_sem=es.at[k],
-            recv_sem=er.at[me_e],
-            device_id={"expert": there},
-            device_id_type=MESH,
-        )
-
-    near_rows = [routed(at_y(o), o - 1) for o in range(1, ny)]
-    far_rows = [routed(far(o), ny - 1 + o) for o in range(ny)]
-
-    @pl.when(me_h == 1)
-    def _():
-        for copy in far_rows:
-            copy.start()
-
-    for copy in near_rows:
-        copy.start()
-    rows_in[me_c, me_e] = rows_out[me_e]
 
     x_order = sorted(range(1, nx), key=lambda o: min(o, nx - o))
     for b, o in enumerate([0] + x_order):
@@ -318,6 +318,16 @@
     own_out = pltpu.make_async_copy(own_grad, rout, local_sem.at[4])
     own_out.start()
 
+    def swap(h, k, sources):
+        for there in sources:
+            came = rows_in.at[me_c, there]
+            pltpu.make_async_copy(came, came, er.at[there]).wait()
+        part = rows_in.at[me_c, pl.ds(pl.multiple_of(h * ny, ny), ny)]
+        remote(part, part, cs.at[k], cr.at[k], sibling)
+
+    sent = len(sends)
+    swap(me_h, 0, [at_y(o) for o in range(1, ny)])
+
     for step in range(2):
         for o in range(1, nx):
             came = recv1.at[o - 1, step]
@@ -340,15 +350,14 @@
                 {"seq": me_x * nz + halves[step] * hz + j},
             )
 
-    for o in range(1, ne):
-        there = (me_e + o) % ne
-        came = rows_in.at[me_c, there]
-        pltpu.make_async_copy(came, came, er.at[there]).wait()
-    remote(rows_in.at[me_c], rows_in.at[me_c], cs.at[0], cr.at[0], sibling)
+    for copy in sends[:sent]:
+        copy.wait_send()
+    swap(1 - me_h, 1, [far(o) for o in range(ny)])
 
     w_copy.wait()
-    other = rows_in.at[1 - me_c]
-    pltpu.make_async_copy(other, other, cr.at[0]).wait()
+    for k, h in enumerate([me_h, 1 - me_h]):
+        other = rows_in.at[1 - me_c, pl.ds(pl.multiple_of(h * ny, ny), ny)]
+        pltpu.make_async_copy(other, other, cr.at[k]).wait()
     hidden = lax.dot_general(
         rows_in[0].reshape(ne * cap, half), w[:, 0:half], NT, preferred_element_type=F32
     )
@@ -374,7 +383,7 @@
     own_out.wait()
     hid_out.wait()
     prompt_out.wait()
-    for copy in sends + near_rows + far_rows:
+    for copy in sends[sent:] + near_rows + far_rows:
         copy.wait_send()
 
 
@@ -441,8 +450,8 @@
             dma((nx - 1,)),
             dma((ne - 1,)),
             dma((ne,)),
-            dma((1,)),
-            dma((1,)),
+            dma((2,)),
+            dma((2,)),
             dma((nx - 1, 2)),
             dma((nx - 1, 2)),
             dma((nz,)),

time: 48.5 us -> 45.3 us (0.934)
  the two profiles are of different devices: /device:TPU:1 before, /device:TPU:480 now
where the time goes in v5:
time: 45.3 us; the launch traced here: 45.2 us
  Pallas kernels  43.9 us (97%)
  between operations  1.29 us (3%)
    pallas_call x1, Pallas kernels, local(): pl.pallas_call(functools.partial(kernel, nx, nz), out_shape=[jax.ShapeDty...  42 us
    pallas_call x1, Pallas kernels, local(): pl.pallas_call(place, out_shape=[jax.ShapeDtypeStruct((toks, 2, HD), F32)...  1.82 us

profile of v5, /device:TPU:480, one launch (start us, length us, event | category | flops | bytes accessed | tf_op | source)
XLA Modules:
  0.0 45.2 jit_solution(1062046174620190358)
XLA Ops:
  1.3 42.0 %moe_attention_backward.1 = (f32[2,32,128]{2,1,0:T(8,128)}, f32[2,128,128]{2,1,0:T(8,128)}, bf16[8,16,768]{2,1,0:T(8,128)(2,1)}) custom-call(s32[1,1]{1,0:T(1,128)S(6)} %copy.13.len_ref, bf16[32,2,128]{2,1,0:T(2,128)(2,1)} %bitcast.22, bf16[128,2,128]{2,1,0:T(2,128)(2,1)} %bitcast.21, s32[8,128]{1,0:T(8,128)} %bitcast.23, f32[8,128]{1,0:T(8,128)} %bitcast.24, ...), custom_call_target="tpu_custom_call" | custom-call | tf_op jit(solution)/shard_map/moe_attention_backward/pallas_call | solution.py:412
  43.3 1.8 %place_outputs.1 = (f32[32,2,128]{2,1,0:T(2,128)}, f32[128,2,128]{2,1,0:T(2,128)}, bf16[8,16,768]{2,1,0:T(8,128)(2,1)}) custom-call(f32[2,32,128]{2,1,0:T(8,128)} %get-tuple-element.9.pin, f32[2,128,128]{2,1,0:T(8,128)} %get-tuple-element.10.rin, bf16[8,16,768]{2,1,0:T(8,128)(2,1)} %get-tuple-element.11.ein), custom_call_target="tpu_custom_call" | custom-call | tf_op jit(solution)/shard_map/place_outputs/pallas_call | solution.py:476

commit v6 on v5

--- a/solution.py
+++ b/solution.py
@@ -211,13 +211,6 @@
     near_rows = [routed(at_y(o), o - 1) for o in range(1, ny)]
     far_rows = [routed(far(o), ny - 1 + o) for o in range(ny)]
 
-    @pl.when(me_h == 1)
-    def _():
-        for copy in far_rows:
-            copy.start()
-
-    for copy in near_rows:
-        copy.start()
     rows_in[me_c, me_e] = rows_out[me_e]
 
     pltpu.make_async_copy(q, q, local_sem.at[0]).wait()
@@ -254,6 +247,11 @@
         block = gath.at[me_x, zb]
         pltpu.make_async_copy(block, block, zr.at[zb]).wait()
         forward(k + 1, zb)
+        if k < ny:
+            pl.when(me_h == 1)(far_rows[k].start)
+
+    for copy in near_rows:
+        copy.start()
 
     x_order = sorted(range(1, nx), key=lambda o: min(o, nx - o))
     for b, o in enumerate([0] + x_order):

time: 45.3 us -> 47.1 us (1.040)
  the two profiles are of different devices: /device:TPU:480 before, /device:TPU:1 now
where the time goes in v6:
time: 47.1 us; the launch traced here: 47 us
  Pallas kernels  45.7 us (97%)
  between operations  1.29 us (3%)
    pallas_call x1, Pallas kernels, local(): pl.pallas_call(functools.partial(kernel, nx, nz), out_shape=[jax.ShapeDty...  43.8 us
    pallas_call x1, Pallas kernels, local(): pl.pallas_call(place, out_shape=[jax.ShapeDtypeStruct((toks, 2, HD), F32)...  1.82 us

profile of v6, /device:TPU:1, one launch (start us, length us, event | category | flops | bytes accessed | tf_op | source)
XLA Modules:
  0.0 47.0 jit_solution(4025323371151376007)
XLA Ops:
  1.3 43.8 %moe_attention_backward.1 = (f32[2,32,128]{2,1,0:T(8,128)}, f32[2,128,128]{2,1,0:T(8,128)}, bf16[8,16,768]{2,1,0:T(8,128)(2,1)}) custom-call(s32[1,1]{1,0:T(1,128)S(6)} %copy.13.len_ref, bf16[32,2,128]{2,1,0:T(2,128)(2,1)} %bitcast.22, bf16[128,2,128]{2,1,0:T(2,128)(2,1)} %bitcast.21, s32[8,128]{1,0:T(8,128)} %bitcast.23, f32[8,128]{1,0:T(8,128)} %bitcast.24, ...), custom_call_target="tpu_custom_call" | custom-call | tf_op jit(solution)/shard_map/moe_attention_backward/pallas_call | solution.py:410
  45.1 1.8 %place_outputs.1 = (f32[32,2,128]{2,1,0:T(2,128)}, f32[128,2,128]{2,1,0:T(2,128)}, bf16[8,16,768]{2,1,0:T(8,128)(2,1)}) custom-call(f32[2,32,128]{2,1,0:T(8,128)} %get-tuple-element.9.pin, f32[2,128,128]{2,1,0:T(8,128)} %get-tuple-element.10.rin, bf16[8,16,768]{2,1,0:T(8,128)(2,1)} %get-tuple-element.11.ein), custom_call_target="tpu_custom_call" | custom-call | tf_op jit(solution)/shard_map/place_outputs/pallas_call | solution.py:474

commit v7 on v6

--- a/solution.py
+++ b/solution.py
@@ -130,8 +130,8 @@
         cols = slice(h * HD, (h + 1) * HD)
         pltpu.make_async_copy(q_hbm.at[:, cols], q.at[h * 128 : (h + 1) * 128], local_sem.at[0]).start()
         pltpu.make_async_copy(g_hbm.at[:, cols], g.at[h * 128 : (h + 1) * 128], local_sem.at[1]).start()
-    w_copy = pltpu.make_async_copy(w_hbm, w, local_sem.at[3])
-    w_copy.start()
+    for k in range(2):
+        pltpu.make_async_copy(w_hbm.at[:, k * half : (k + 1) * half], w.at[k], local_sem.at[3]).start()
     small[0].wait()
     gath[me_x, me_z, 0] = pkv_ref[:, 0, :]
     gath[me_x, me_z, 1] = pkv_ref[:, 1, :]
@@ -242,13 +242,16 @@
     small[3].wait()
     forward_block(own_b, rkv_ref[:, 0, :], rkv_ref[:, 1, :], True)
 
+    @pl.when(me_h == 1)
+    def _():
+        for copy in far_rows:
+            copy.start()
+
     for k, o in enumerate(z_order):
         zb = (me_z + o) % nz
         block = gath.at[me_x, zb]
         pltpu.make_async_copy(block, block, zr.at[zb]).wait()
         forward(k + 1, zb)
-        if k < ny:
-            pl.when(me_h == 1)(far_rows[k].start)
 
     for copy in near_rows:
         copy.start()
@@ -352,16 +355,18 @@
         copy.wait_send()
     swap(1 - me_h, 1, [far(o) for o in range(ny)])
 
-    w_copy.wait()
+    pltpu.make_async_copy(w, w, local_sem.at[3]).wait()
+
+    def product(c):
+        return lax.dot_general(
+            rows_in[c].reshape(ne * cap, half), w[c], NT, preferred_element_type=F32
+        )
+
+    hidden = product(me_c)
     for k, h in enumerate([me_h, 1 - me_h]):
         other = rows_in.at[1 - me_c, pl.ds(pl.multiple_of(h * ny, ny), ny)]
         pltpu.make_async_copy(other, other, cr.at[k]).wait()
-    hidden = lax.dot_general(
-        rows_in[0].reshape(ne * cap, half), w[:, 0:half], NT, preferred_element_type=F32
-    )
-    hidden = hidden + lax.dot_general(
-        rows_in[1].reshape(ne * cap, half), w[:, half : 2 * half], NT, preferred_element_type=F32
-    )
+    hidden = hidden + product(1 - me_c)
     hid[...] = hidden.astype(BF16).reshape(hid.shape)
     hid_out = pltpu.make_async_copy(hid, eout, local_sem.at[5])
     hid_out.start()
@@ -420,7 +425,7 @@
             pltpu.VMEM((heads * rows, HD), BF16),
             pltpu.VMEM((heads * rows, HD), BF16),
             pltpu.VMEM((rows, half), BF16),
-            pltpu.VMEM((hidden, features), BF16),
+            pltpu.VMEM((2, hidden, half), BF16),
             pltpu.VMEM((nx, nz, 2, toks, HD), BF16),
             pltpu.VMEM((nx + 1, max(blk, rows), heads * rows), F32),
             pltpu.VMEM((nx + 1, max(blk, rows), heads * rows), F32),

time: 47.1 us -> 44.8 us (0.951)
  the two profiles are of different devices: /device:TPU:1 before, /device:TPU:6 now
where the time goes in v7:
time: 44.8 us; the launch traced here: 44.6 us
  Pallas kernels  43.3 us (97%)
  between operations  1.29 us (3%)
    pallas_call x1, Pallas kernels, local(): pl.pallas_call(functools.partial(kernel, nx, nz), out_shape=[jax.ShapeDty...  41.5 us
    pallas_call x1, Pallas kernels, local(): pl.pallas_call(place, out_shape=[jax.ShapeDtypeStruct((toks, 2, HD), F32)...  1.82 us

profile of v7, /device:TPU:6, one launch (start us, length us, event | category | flops | bytes accessed | tf_op | source)
XLA Modules:
  0.0 44.6 jit_solution(8505471812431729826)
XLA Ops:
  1.3 41.5 %moe_attention_backward.1 = (f32[2,32,128]{2,1,0:T(8,128)}, f32[2,128,128]{2,1,0:T(8,128)}, bf16[8,16,768]{2,1,0:T(8,128)(2,1)}) custom-call(s32[1,1]{1,0:T(1,128)S(6)} %copy.13.len_ref, bf16[32,2,128]{2,1,0:T(2,128)(2,1)} %bitcast.22, bf16[128,2,128]{2,1,0:T(2,128)(2,1)} %bitcast.21, s32[8,128]{1,0:T(8,128)} %bitcast.23, f32[8,128]{1,0:T(8,128)} %bitcast.24, ...), custom_call_target="tpu_custom_call" | custom-call | tf_op jit(solution)/shard_map/moe_attention_backward/pallas_call | solution.py:415
  42.8 1.8 %place_outputs.1 = (f32[32,2,128]{2,1,0:T(2,128)}, f32[128,2,128]{2,1,0:T(2,128)}, bf16[8,16,768]{2,1,0:T(8,128)(2,1)}) custom-call(f32[2,32,128]{2,1,0:T(8,128)} %get-tuple-element.9.pin, f32[2,128,128]{2,1,0:T(8,128)} %get-tuple-element.10.rin, bf16[8,16,768]{2,1,0:T(8,128)(2,1)} %get-tuple-element.11.ein), custom_call_target="tpu_custom_call" | custom-call | tf_op jit(solution)/shard_map/place_outputs/pallas_call | solution.py:479

commit v8 on v7

--- a/solution.py
+++ b/solution.py
@@ -213,13 +213,6 @@
 
     rows_in[me_c, me_e] = rows_out[me_e]
 
-    pltpu.make_async_copy(q, q, local_sem.at[0]).wait()
-    pltpu.make_async_copy(g, g, local_sem.at[1]).wait()
-    row_at = lax.broadcasted_iota(jnp.int32, (128, HD), 0)
-    for h in range(heads):
-        part = g[h * 128 : (h + 1) * 128, :]
-        g[h * 128 : (h + 1) * 128, :] = jnp.where(row_at < length, part.astype(F32), 0.0).astype(BF16)
-
     def forward_block(b, keys, values, causal):
         n = keys.shape[0]
         for t in range(rows_all // TILE):
@@ -239,8 +232,17 @@
             prob[b, 0:n, rows] = probs
 
     own_b = nx
-    small[3].wait()
-    forward_block(own_b, rkv_ref[:, 0, :], rkv_ref[:, 1, :], True)
+
+    def own_scores():
+        pltpu.make_async_copy(q, q, local_sem.at[0]).wait()
+        pltpu.make_async_copy(g, g, local_sem.at[1]).wait()
+        row_at = lax.broadcasted_iota(jnp.int32, (128, HD), 0)
+        for h in range(heads):
+            part = g[h * 128 : (h + 1) * 128, :]
+            g[h * 128 : (h + 1) * 128, :] = jnp.where(row_at < length, part.astype(F32), 0.0).astype(BF16)
+
+        small[3].wait()
+        forward_block(own_b, rkv_ref[:, 0, :], rkv_ref[:, 1, :], True)
 
     @pl.when(me_h == 1)
     def _():
@@ -252,6 +254,8 @@
         block = gath.at[me_x, zb]
         pltpu.make_async_copy(block, block, zr.at[zb]).wait()
         forward(k + 1, zb)
+        if k == min(1, nz - 2):
+            own_scores()
 
     for copy in near_rows:
         copy.start()
@@ -295,29 +299,54 @@
     sub = hz * toks
     my_half, my_at = me_z // hz, me_z % hz
     halves = [1 - my_half, my_half]
-    for step in range(2):
-        keys = pl.ds(pl.multiple_of(halves[step] * sub, sub), sub)
+    pair = max(hz // 2, 1)
+    steps = [(0, j, pair) for j in range(0, hz, pair)] + [(1, 0, hz)]
+    mine = pl.ds(pl.multiple_of(my_at * toks, toks), toks)
+
+    def produce(step):
+        side, j0, nj = steps[step]
+        n = nj * toks
+        keys = pl.ds(pl.multiple_of(halves[side] * sub + j0 * toks, n), n)
+        at = slice(j0 * toks, j0 * toks + n)
         for b, o in reversed(list(enumerate([0] + x_order))):
-            grad_k, grad_v = backward_block(b, keys, sub, b % 2)
+            grad_k, grad_v = backward_block(b, keys, n, b % 2)
             if o:
-                part1[b - 1, step, 0] = grad_k.astype(BF16)
-                part1[b - 1, step, 1] = grad_v.astype(BF16)
+                part1[b - 1, side, 0, at, :] = grad_k.astype(BF16)
+                part1[b - 1, side, 1, at, :] = grad_v.astype(BF16)
                 remote(
-                    part1.at[b - 1, step],
-                    recv1.at[o - 1, step],
+                    part1.at[b - 1, side, :, at],
+                    recv1.at[o - 1, side, :, at],
                     s1.at[o - 1, step],
                     r1.at[o - 1, step],
                     at_x(nx - o),
                 )
             else:
-                own_sum[step, 0] = grad_k
-                own_sum[step, 1] = grad_v
-
-    grad_k, grad_v = backward_block(own_b, slice(0, 128), 128, 1)
-    own_grad[0] = grad_k
-    own_grad[1] = grad_v
-    own_out = pltpu.make_async_copy(own_grad, rout, local_sem.at[4])
-    own_out.start()
+                own_sum[side, 0, at, :] = grad_k
+                own_sum[side, 1, at, :] = grad_v
+
+    def pass_on(step):
+        side, j0, nj = steps[step]
+        at = slice(j0 * toks, (j0 + nj) * toks)
+        for o in range(1, nx):
+            came = recv1.at[o - 1, side, :, at]
+            pltpu.make_async_copy(came, came, r1.at[o - 1, step]).wait()
+        for j in range(j0, j0 + nj):
+            keys = slice(j * toks, (j + 1) * toks)
+            for kv in range(2):
+                total = own_sum[side, kv, keys, :]
+                for o in range(1, nx):
+                    total = total + recv1[o - 1, side, kv, keys, :].astype(F32)
+                own_sum[side, kv, keys, :] = total
+                part2[side, j, kv] = total.astype(BF16)
+        for o in range(side, nj):
+            j = j0 + (my_at + o) % nj
+            remote(
+                part2.at[side, j],
+                recv2.at[me_z],
+                s2.at[side * hz + j0 + o],
+                r2.at[me_z],
+                {"seq": me_x * nz + halves[side] * hz + j},
+            )
 
     def swap(h, k, sources):
         for there in sources:
@@ -326,30 +355,19 @@
         part = rows_in.at[me_c, pl.ds(pl.multiple_of(h * ny, ny), ny)]
         remote(part, part, cs.at[k], cr.at[k], sibling)
 
+    for step in range(len(steps) - 1):
+        produce(step)
     sent = len(sends)
+    grad_k, grad_v = backward_block(own_b, slice(0, 128), 128, 1)
+    own_grad[0] = grad_k
+    own_grad[1] = grad_v
+    own_out = pltpu.make_async_copy(own_grad, rout, local_sem.at[4])
+    own_out.start()
+    pass_on(0)
+    produce(len(steps) - 1)
     swap(me_h, 0, [at_y(o) for o in range(1, ny)])
-
-    for step in range(2):
-        for o in range(1, nx):
-            came = recv1.at[o - 1, step]
-            pltpu.make_async_copy(came, came, r1.at[o - 1, step]).wait()
-        for j in range(hz):
-            keys = slice(j * toks, (j + 1) * toks)
-            for kv in range(2):
-                total = own_sum[step, kv, keys, :]
-                for o in range(1, nx):
-                    total = total + recv1[o - 1, step, kv, keys, :].astype(F32)
-                own_sum[step, kv, keys, :] = total
-                part2[step, j, kv] = total.astype(BF16)
-        for o in range(step, hz):
-            j = (my_at + o) % hz
-            remote(
-                part2.at[step, j],
-                recv2.at[me_z],
-                s2.at[step * hz + o],
-                r2.at[me_z],
-                {"seq": me_x * nz + halves[step] * hz + j},
-            )
+    for step in range(1, len(steps)):
+        pass_on(step)
 
     for copy in sends[:sent]:
         copy.wait_send()
@@ -455,8 +473,8 @@
             dma((ne,)),
             dma((2,)),
             dma((2,)),
-            dma((nx - 1, 2)),
-            dma((nx - 1, 2)),
+            dma((nx - 1, 3)),
+            dma((nx - 1, 3)),
             dma((nz,)),
             dma((nz,)),
             pltpu.SemaphoreType.REGULAR,

time: 44.8 us -> 49.3 us (1.10)
  the two profiles are of different devices: /device:TPU:6 before, /device:TPU:480 now
where the time goes in v8:
time: 49.3 us; the launch traced here: 49.1 us
  Pallas kernels  47.8 us (97%)
  between operations  1.29 us (3%)
    pallas_call x1, Pallas kernels, local(): pl.pallas_call(functools.partial(kernel, nx, nz), out_shape=[jax.ShapeDty...  46 us
    pallas_call x1, Pallas kernels, local(): pl.pallas_call(place, out_shape=[jax.ShapeDtypeStruct((toks, 2, HD), F32)...  1.82 us

profile of v8, /device:TPU:480, one launch (start us, length us, event | category | flops | bytes accessed | tf_op | source)
XLA Modules:
  0.0 49.1 jit_solution(3202791297199562278)
XLA Ops:
  1.3 46.0 %moe_attention_backward.1 = (f32[2,32,128]{2,1,0:T(8,128)}, f32[2,128,128]{2,1,0:T(8,128)}, bf16[8,16,768]{2,1,0:T(8,128)(2,1)}) custom-call(s32[1,1]{1,0:T(1,128)S(6)} %copy.13.len_ref, bf16[32,2,128]{2,1,0:T(2,128)(2,1)} %bitcast.22, bf16[128,2,128]{2,1,0:T(2,128)(2,1)} %bitcast.21, s32[8,128]{1,0:T(8,128)} %bitcast.23, f32[8,128]{1,0:T(8,128)} %bitcast.24, ...), custom_call_target="tpu_custom_call" | custom-call | tf_op jit(solution)/shard_map/moe_attention_backward/pallas_call | solution.py:433
  47.3 1.8 %place_outputs.1 = (f32[32,2,128]{2,1,0:T(2,128)}, f32[128,2,128]{2,1,0:T(2,128)}, bf16[8,16,768]{2,1,0:T(8,128)(2,1)}) custom-call(f32[2,32,128]{2,1,0:T(8,128)} %get-tuple-element.9.pin, f32[2,128,128]{2,1,0:T(8,128)} %get-tuple-element.10.rin, bf16[8,16,768]{2,1,0:T(8,128)(2,1)} %get-tuple-element.11.ein), custom_call_target="tpu_custom_call" | custom-call | tf_op jit(solution)/shard_map/place_outputs/pallas_call | solution.py:497

commit v9 on v7

--- a/solution.py
+++ b/solution.py
@@ -242,16 +242,21 @@
     small[3].wait()
     forward_block(own_b, rkv_ref[:, 0, :], rkv_ref[:, 1, :], True)
 
-    @pl.when(me_h == 1)
-    def _():
-        for copy in far_rows:
-            copy.start()
+    def far_start(core):
+        @pl.when((me_h == 1) & (me_c == core))
+        def _():
+            for copy in far_rows:
+                copy.start()
+
+    far_start(0)
 
     for k, o in enumerate(z_order):
         zb = (me_z + o) % nz
         block = gath.at[me_x, zb]
         pltpu.make_async_copy(block, block, zr.at[zb]).wait()
         forward(k + 1, zb)
+        if k == 0:
+            far_start(1)
 
     for copy in near_rows:
         copy.start()

time: 44.8 us -> 44.9 us (level)
  no operation moved by 1% of the time
where the time goes in v9:
time: 44.9 us; the launch traced here: 44.7 us
  Pallas kernels  43.4 us (97%)
  between operations  1.29 us (3%)
    pallas_call x1, Pallas kernels, local(): pl.pallas_call(functools.partial(kernel, nx, nz), out_shape=[jax.ShapeDty...  41.6 us
    pallas_call x1, Pallas kernels, local(): pl.pallas_call(place, out_shape=[jax.ShapeDtypeStruct((toks, 2, HD), F32)...  1.82 us

profile of v9, /device:TPU:6, one launch (start us, length us, event | category | flops | bytes accessed | tf_op | source)
XLA Modules:
  0.0 44.7 jit_solution(453104963280286919)
XLA Ops:
  1.3 41.6 %moe_attention_backward.1 = (f32[2,32,128]{2,1,0:T(8,128)}, f32[2,128,128]{2,1,0:T(8,128)}, bf16[8,16,768]{2,1,0:T(8,128)(2,1)}) custom-call(s32[1,1]{1,0:T(1,128)S(6)} %copy.13.len_ref, bf16[32,2,128]{2,1,0:T(2,128)(2,1)} %bitcast.22, bf16[128,2,128]{2,1,0:T(2,128)(2,1)} %bitcast.21, s32[8,128]{1,0:T(8,128)} %bitcast.23, f32[8,128]{1,0:T(8,128)} %bitcast.24, ...), custom_call_target="tpu_custom_call" | custom-call | tf_op jit(solution)/shard_map/moe_attention_backward/pallas_call | solution.py:420
  42.9 1.8 %place_outputs.1 = (f32[32,2,128]{2,1,0:T(2,128)}, f32[128,2,128]{2,1,0:T(2,128)}, bf16[8,16,768]{2,1,0:T(8,128)(2,1)}) custom-call(f32[2,32,128]{2,1,0:T(8,128)} %get-tuple-element.9.pin, f32[2,128,128]{2,1,0:T(8,128)} %get-tuple-element.10.rin, bf16[8,16,768]{2,1,0:T(8,128)(2,1)} %get-tuple-element.11.ein), custom_call_target="tpu_custom_call" | custom-call | tf_op jit(solution)/shard_map/place_outputs/pallas_call | solution.py:484
